TPU v7x, 512 devices: a whole 4x8x8 slice. The times are simulated.
512 devices in a mesh: row: 16 (over z_lo, x), col: 16 (over y, z_hi), cond: 2 (over core).
Axes of the slice: x: 4, y: 8, z: 8 (z_hi: 2, z_lo: 4; z = z_hi * 4 + z_lo), core: 2. Of those that a mesh axis runs over, the one named last changes fastest.
Arguments:
- mask: float32 [2048, 2048], P('row', 'col'), may hold values from -1 to 1
- target: int32 [2048, 2048], P('row', 'col'), may hold values 0 or 1
- cond_index: int32 [4], P('cond'), may hold values from 0 to 7
- kernels: float32 [8, 2, 12, 576], replicated, may hold values from -6 to 6
- dose: float32 [8], replicated, may hold values from 0.7 to 1.4
Outputs:
- mask_grad: float32 [2048, 2048], P('row', 'col')
All inputs are finite; a program needn't handle non-finite values. No bound on the sum of `target` on one device may be relied on, other than what follows from the above.
Results may differ from a plain program's by a relative error of at most 0.0003.
Values sent between devices are 32-bit elements; how exact they have to be, the bound alone decides.
A program may use at most 64 MiB of HBM per device.

v0:
```python
import math
import jax
import jax.numpy as jnp
from jax import lax
from jax.sharding import PartitionSpec as P

MARGIN = 128
BAND = 24
STEEP = 4.0
THRESH = 0.6


def extended(block, sides, width):
    for axis, dim in sides:
        count = lax.axis_size(axis)
        forward = [(i, i + 1) for i in range(count - 1)]
        backward = [(target, source) for source, target in forward]
        low = lax.ppermute(
            lax.slice_in_dim(block, block.shape[dim] - width, None, axis=dim), axis, forward
        )
        high = lax.ppermute(lax.slice_in_dim(block, 0, width, axis=dim), axis, backward)
        block = jnp.concatenate([low, block, high], axis=dim)
    return block


def highest(left_side, right_side):
    return jnp.dot(
        left_side, right_side, precision=lax.Precision.HIGHEST, preferred_element_type=jnp.float32
    )


def tables(length, start, window_size, band_size):
    frequency = jnp.arange(band_size, dtype=jnp.int32) - band_size // 2
    positions = jnp.arange(length, dtype=jnp.int32) + start
    phases = frequency[:, None] * positions[None, :] % window_size
    angles = phases.astype(jnp.float32) * (2.0 * math.pi / window_size)
    return (jnp.cos(angles), jnp.sin(angles))


def row_product(segment, row_start, window_size, band_size):
    cosine_table, sine_table = tables(segment.shape[0], row_start, window_size, band_size)
    return highest(jnp.concatenate([cosine_table, sine_table], axis=0), segment)


def col_product(partial_rows, col_start, window_size, band_size):
    cosine_table, sine_table = tables(partial_rows.shape[1], col_start, window_size, band_size)
    products = highest(partial_rows, jnp.concatenate([cosine_table, sine_table], axis=0).T)
    upper_cos = products[:band_size, :band_size]
    upper_sin = products[:band_size, band_size:]
    lower_cos = products[band_size:, :band_size]
    lower_sin = products[band_size:, band_size:]
    return jnp.stack([upper_cos - lower_sin, -lower_cos - upper_sin]) / window_size


def tile_loss(spectrum, kernel, dose_value, goal_map):
    tile_size = goal_map.shape[0]
    band_size = spectrum.shape[1]
    window_size = tile_size + 2 * MARGIN
    kernel_real = kernel[0].reshape(-1, band_size, band_size)
    kernel_imag = kernel[1].reshape(-1, band_size, band_size)
    kernel_count = kernel_real.shape[0]
    product_real = kernel_real * spectrum[0] - kernel_imag * spectrum[1]
    product_imag = kernel_real * spectrum[1] + kernel_imag * spectrum[0]
    stacked = jnp.concatenate([product_real, product_imag], axis=1)
    stacked = jnp.transpose(stacked, (1, 0, 2)).reshape(2 * band_size, kernel_count * band_size)
    cosine_table, sine_table = tables(tile_size, MARGIN, window_size, band_size)
    cosine_cols = cosine_table.T
    sine_cols = sine_table.T
    inverse_left = jnp.concatenate(
        [
            jnp.concatenate([cosine_cols, -sine_cols], 1),
            jnp.concatenate([sine_cols, cosine_cols], 1),
        ],
        0,
    )
    partial_rows = highest(inverse_left, stacked)
    rows_real = partial_rows[:tile_size].reshape(tile_size, kernel_count, band_size)
    rows_imag = partial_rows[tile_size:].reshape(tile_size, kernel_count, band_size)
    rows_both = jnp.concatenate([rows_real, rows_imag], axis=2)
    rows_both = jnp.transpose(rows_both, (1, 0, 2)).reshape(kernel_count * tile_size, 2 * band_size)
    inverse_right = jnp.concatenate(
        [
            jnp.concatenate([cosine_table, sine_table], 1),
            jnp.concatenate([-sine_table, cosine_table], 1),
        ],
        0,
    )
    fields = highest(rows_both, inverse_right)
    squared = (fields * fields).reshape(kernel_count, tile_size, 2, tile_size)
    intensity = jnp.sum(squared, axis=(0, 2)) / (kernel_count * band_size * band_size)
    resist = jax.nn.sigmoid(STEEP * (dose_value * intensity - THRESH))
    return jnp.sum(jnp.square(resist - goal_map))


def interior_adjoint(cotangent, tile_size, window_size):
    band_size = cotangent.shape[1]
    cosine_table, sine_table = tables(tile_size, MARGIN, window_size, band_size)
    joined = jnp.concatenate([cotangent[0], cotangent[1]], axis=1)
    right_side = jnp.concatenate(
        [
            jnp.concatenate([cosine_table, -sine_table], 1),
            jnp.concatenate([-sine_table, -cosine_table], 1),
        ],
        0,
    )
    halves = highest(joined, right_side)
    stacked = jnp.concatenate([halves[:, :tile_size], halves[:, tile_size:]], axis=0)
    left_side = jnp.concatenate([cosine_table, sine_table], axis=0).T
    return highest(left_side, stacked) / window_size


def shards(mask, target, cond_index, kernels, dose):
    tile_size = mask.shape[0]
    window_size = tile_size + 2 * MARGIN
    window = extended(mask, (("row", 0), ("col", 1)), MARGIN)
    spectrum = col_product(row_product(window, 0, window_size, BAND), 0, window_size, BAND)
    goal_map = target.astype(jnp.float32)
    summed = jnp.zeros((2, BAND, BAND), jnp.float32)
    for ordinal in range(cond_index.shape[0]):
        setting = cond_index[ordinal]
        kernel = lax.dynamic_index_in_dim(kernels, setting, 0, keepdims=False)
        dose_value = lax.dynamic_index_in_dim(dose, setting, 0, keepdims=False)
        summed = summed + jax.grad(tile_loss)(spectrum, kernel, dose_value, goal_map)
    local_terms = interior_adjoint(summed, tile_size, window_size)
    return lax.psum(local_terms, "cond")


def solution(mesh):
    in_specs = (P("row", "col"), P("row", "col"), P("cond"), P(), P())
    out_specs = P("row", "col")
    return jax.shard_map(shards, mesh=mesh, in_specs=in_specs, out_specs=out_specs, check_vma=False)
```

profile of v0, /device:TPU:1, one launch (start us, length us, event | category | flops | bytes accessed | tf_op | source)
XLA Modules:
  0.0 131.9 jit_solution(18439680603129885286)
XLA Ops:
  6.5 3.9 %collective-permute-start = (f32[128,128]{1,0:T(8,128)}, f32[128,128]{1,0:T(8,128)S(1)}, u32[]{:S(2)}, u32[]{:S(2)}) collective-permute-start(f32[128,128]{1,0:T(8,128)} %param.5), channel_id=1, source_target_pairs={{0,32},{32,64},{64,96},{96,128},{128,160},{160,192},{192,224},{224... | collective-permute-start | bytes 196616 | tf_op jit(solution)/shard_map/ppermute | solution.py:18
  10.5 1.3 collective-permute-start.1
  11.8 0.2 fusion.44
  12.0 0.1 fusion.77
  12.2 1.3 %fusion.100 = (s32[1]{0:T(128)}, s32[1]{0:T(128)}) fusion(s32[2]{0:T(128)} %param.7), kind=kLoop, calls=%fused_computation.146 | loop fusion | bytes 16 | tf_op jit(solution)/shard_map/slice | solution.py:120
  17.5 1.4 %fusion.99 = (f32[1]{0:T(128)}, f32[1]{0:T(128)}) fusion(f32[8]{0:T(128)} %param.9, s32[]{:T(128)S(6)} %select_n.60, s32[]{:T(128)S(6)} %select_n.63), kind=kLoop, calls=%fused_computation.145 | loop fusion | bytes 24 | tf_op jit(solution)/shard_map/jit(dynamic_index_in_dim)/dynamic_slice | solution.py:122
  21.6 1.3 dynamic-slice_reduce_fusion.3
  22.9 0.1 squeeze.31
  23.0 0.1 squeeze.32
  23.1 0.1 squeeze.34
  23.2 0.1 squeeze.35
  23.4 0.8 constant_dynamic-update-slice_fusion.1
  24.2 10.6 %collective-permute-start.2 = (f32[384,128]{1,0:T(8,128)S(1)}, f32[384,128]{1,0:T(8,128)S(1)}, u32[]{:S(2)}, u32[]{:S(2)}) collective-permute-start(f32[384,128]{1,0:T(8,128)S(1)} %constant_dynamic-update-slice_fusion), channel_id=1, source_target_pairs={{0,2},{2,4},{4,6},{6,8},{8,10},{10,12},{12,14},{14,16},{16,18},{18... | collective-permute-start | bytes 589832 | tf_op jit(solution)/shard_map/ppermute | solution.py:18
  34.9 1.3 collective-permute-start.3
  36.2 0.1 fusion.79
  36.3 1.8 %collective-permute-done.2 = f32[384,128]{1,0:T(8,128)S(1)} collective-permute-done((f32[384,128]{1,0:T(8,128)S(1)}, f32[384,128]{1,0:T(8,128)S(1)}, u32[]{:S(2)}, u32[]{:S(2)}) %collective-permute-start.2) | collective-permute-done | bytes 196640 | tf_op jit(solution)/shard_map/ppermute | solution.py:18
  38.1 7.9 %collective-permute-done.3 = f32[384,128]{1,0:T(8,128)S(1)} collective-permute-done((f32[384,128]{1,0:T(8,128)S(1)}, f32[384,128]{1,0:T(8,128)S(1)}, u32[]{:S(2)}, u32[]{:S(2)}) %collective-permute-start.3) | collective-permute-done | bytes 196640 | tf_op jit(solution)/shard_map/ppermute | solution.py:21
  46.0 0.4 fusion.6
  46.5 0.2 fusion.32
  46.7 0.1 fusion.57
  46.8 0.1 multiply_subtract_fusion.1
  46.9 0.8 maximum_bitcast_fusion
  47.6 0.1 copy.35
  47.7 0.4 fusion.71
  48.3 2.6 %fusion.102 = (f32[1536,256]{1,0:T(8,128)}, f32[1536,256]{1,0:T(8,128)S(1)}) fusion(f32[24,128]{1,0:T(8,128)S(1)} %get-tuple-element.51, f32[24,128]{1,0:T(8,128)S(1)} %get-tuple-element.49, f32[24,128]{1,0:T(8,128)S(1)} %get-tuple-element.50, f32[6,8,12,128]{3,2,1,0:T(8,128)S(1)} %bitcast.85), kind=kOutput, calls=%fused_computation.148 | convolution fusion | flops 226922496 | bytes 3477504 | tf_op jit(solution)/shard_map/jvp()/dot_general | solution.py:27
  50.9 2.1 %reshape.142 = f32[12,128,2,128]{3,2,1,0:T(2,128)S(1)} reshape(f32[1536,256]{1,0:T(8,128)} %get-tuple-element.60) | data formatting | bytes 3145728 | tf_op jit(solution)/shard_map/jvp()/reshape | solution.py:89
  53.0 1.7 %copy.28 = f32[48,12,24]{0,2,1:T(8,128)} copy(f32[48,12,24]{2,0,1:T(8,128)} %get-tuple-element.62) | data formatting | bytes 110592 | tf_op jit(solution)/shard_map/jvp()/transpose | solution.py:65
  54.7 1.3 fusion.72
  56.1 3.1 %fusion.101 = (f32[1536,256]{1,0:T(8,128)}, f32[1536,256]{1,0:T(8,128)}) fusion(f32[24,128]{1,0:T(8,128)S(1)} %get-tuple-element.51, f32[24,128]{1,0:T(8,128)S(1)} %get-tuple-element.49, f32[24,128]{1,0:T(8,128)S(1)} %get-tuple-element.50, f32[6,8,12,128]{3,2,1,0:T(8,128)S(1)} %bitcast.86), kind=kOutput, calls=%fused_computation.147 | convolution fusion | flops 226922496 | bytes 3477504 | tf_op jit(solution)/shard_map/jvp()/dot_general | solution.py:27
  59.3 2.9 %reshape.128 = f32[12,128,2,128]{3,2,1,0:T(2,128)} reshape(f32[1536,256]{1,0:T(8,128)} %get-tuple-element.58) | data formatting | bytes 3145728 | tf_op jit(solution)/shard_map/jvp()/reshape | solution.py:89
  62.1 1.3 reduce_sum.97
  63.4 2.7 %reduce_sum.86 = f32[128,128]{1,0:T(8,128)} reduce(f32[12,128,2,128]{3,2,1,0:T(2,128)} %reshape.128, f32[]{:T(128)} %constant.70.clone.1), dimensions={0,2}, to_apply=%region_0.1 | reduce | flops 376832 | bytes 1638404 | tf_op jit(solution)/shard_map/jvp()/reduce_sum | solution.py:90
  66.1 1.6 %fusion.28 = (f32[128,128]{1,0:T(8,128)S(1)}, f32[128,128]{1,0:T(8,128)}) fusion(s32[128,128]{1,0:T(8,128)} %param.6, f32[128,128]{1,0:T(8,128)} %reduce_sum.86, f32[]{:T(128)} %bitcast.11, f32[]{:T(128)} %bitcast.10, f32[]{:T(128)} %bitcast.28, f32[128,128]{1,0:T(8,128)} %reduce_sum.97, f32[]{:T(128)} %bitcast.27), kind=kLoop, calls=%fused_computation.50 | loop fusion | flops 442368 | bytes 327696 | tf_op jit(solution)/shard_map/transpose(jvp())/div | solution.py:90
  67.7 0.5 broadcast_in_dim.4
  68.2 2.4 %fusion.2 = f32[1536,48]{0,1:T(8,128)} fusion(f32[192,8,2,128]{3,2,1,0:T(2,128)S(1)} %bitcast.81, f32[1536,256]{1,0:T(8,128)S(1)} %copy-done, f32[24,128]{1,0:T(8,128)S(1)} %get-tuple-element.51, f32[24,128]{1,0:T(8,128)S(1)} %get-tuple-element.49, f32[24,128]{1,0:T(8,128)S(1)} %get-tuple-element.50), kind=kOutput, calls=%fused_computation.4 | convolution fusion | flops 227315712 | bytes 3477504 | tf_op jit(solution)/shard_map/transpose(jvp())/dot_general | solution.py:27
  70.7 1.1 reshape.130
  71.9 0.4 fusion.22
  72.3 0.1 copy.34
  72.5 0.1 multiply_reduce_fusion.7
  72.6 0.5 broadcast_in_dim.5
  73.1 1.7 %fusion = f32[1536,48]{0,1:T(8,128)S(1)} fusion(f32[192,8,2,128]{3,2,1,0:T(2,128)S(1)} %bitcast.82, f32[1536,256]{1,0:T(8,128)S(1)} %get-tuple-element.61, f32[24,128]{1,0:T(8,128)S(1)} %get-tuple-element.51, f32[24,128]{1,0:T(8,128)S(1)} %get-tuple-element.49, f32[24,128]{1,0:T(8,128)S(1)} %get-tuple-element.50), kind=kOutput, calls=%fused_computation.1 | convolution fusion | flops 227315712 | bytes 3477504 | tf_op jit(solution)/shard_map/transpose(jvp())/dot_general | solution.py:27
  75.1 0.4 fusion.18
  75.5 0.1 copy.41
  75.6 0.1 multiply_reduce_fusion.3
  75.7 0.2 fusion.35
  76.0 0.9 convolution_multiply_fusion
  76.9 46.6 %all-reduce.14.cloned.1.call-done = f32[128,128]{1,0:T(8,128)} async-done(((f32[128,128]{1,0:T(8,128)}), f32[128,128]{1,0:T(8,128)}) %all-reduce.14.cloned.1.call-update) | async-done | bytes 65552 | tf_op jit(solution)/shard_map/psum | solution.py:125
  123.6 1.5 %copy.71 = f32[128,128]{1,0:T(8,128)} copy(f32[128,128]{1,0:T(8,128)} %all-reduce.14.cloned.1.call-done) | data formatting | bytes 131072
  (40 shorter events, 0.7 us)
Async XLA Ops:
  6.5 117.0 %all-reduce.14.cloned.1.call-start = ((), (), s32[]{:S(2)}) async-start(), calls=%async_computation | async-start | bytes 131072 | tf_op jit(solution)/shard_map/psum | solution.py:125
  6.5 16.8 %collective-permute-start = (f32[128,128]{1,0:T(8,128)}, f32[128,128]{1,0:T(8,128)S(1)}, u32[]{:S(2)}, u32[]{:S(2)}) collective-permute-start(f32[128,128]{1,0:T(8,128)} %param.5), channel_id=1, source_target_pairs={{0,32},{32,64},{64,96},{96,128},{128,160},{160,192},{192,224},{224... | collective-permute-start | bytes 196616 | tf_op jit(solution)/shard_map/ppermute | solution.py:18
  10.5 13.7 %collective-permute-start.1 = (f32[128,128]{1,0:T(8,128)}, f32[128,128]{1,0:T(8,128)S(1)}, u32[]{:S(2)}, u32[]{:S(2)}) collective-permute-start(f32[128,128]{1,0:T(8,128)} %param.5), channel_id=1, source_target_pairs={{32,0},{64,32},{96,64},{128,96},{160,128},{192,160},{224,192},{256... | collective-permute-start | bytes 196616 | tf_op jit(solution)/shard_map/ppermute | solution.py:21
  23.0 23.9 %copy-start.1 = (f32[12,24,24]{2,1,0:T(8,128)}, f32[12,24,24]{2,1,0:T(8,128)S(1)}, u32[]{:S(2)}) copy-start(f32[12,24,24]{2,1,0:T(8,128)S(1)} %squeeze.31) | copy-start | bytes 82948
  23.1 23.8 %copy-start.3 = (f32[12,24,24]{2,1,0:T(8,128)}, f32[12,24,24]{2,1,0:T(8,128)S(1)}, u32[]{:S(2)}) copy-start(f32[12,24,24]{2,1,0:T(8,128)S(1)} %squeeze.32) | copy-start | bytes 82948
  24.2 13.9 %collective-permute-start.2 = (f32[384,128]{1,0:T(8,128)S(1)}, f32[384,128]{1,0:T(8,128)S(1)}, u32[]{:S(2)}, u32[]{:S(2)}) collective-permute-start(f32[384,128]{1,0:T(8,128)S(1)} %constant_dynamic-update-slice_fusion), channel_id=1, source_target_pairs={{0,2},{2,4},{4,6},{6,8},{8,10},{10,12},{12,14},{14,16},{16,18},{18... | collective-permute-start | bytes 589832 | tf_op jit(solution)/shard_map/ppermute | solution.py:18
  34.9 11.1 %collective-permute-start.3 = (f32[384,128]{1,0:T(8,128)S(1)}, f32[384,128]{1,0:T(8,128)S(1)}, u32[]{:S(2)}, u32[]{:S(2)}) collective-permute-start(f32[384,128]{1,0:T(8,128)S(1)} %constant_dynamic-update-slice_fusion), channel_id=1, source_target_pairs={{2,0},{4,2},{6,4},{8,6},{10,8},{12,10},{14,12},{16,14},{18,16},{20... | collective-permute-start | bytes 589832 | tf_op jit(solution)/shard_map/ppermute | solution.py:21
  63.4 4.8 %copy-start = (f32[1536,256]{1,0:T(8,128)S(1)}, f32[1536,256]{1,0:T(8,128)}, u32[]{:S(2)}) copy-start(f32[1536,256]{1,0:T(8,128)} %get-tuple-element.59) | copy-start | bytes 4718596
  70.7 1.8 %copy-start.2 = (f32[12,24,24]{2,1,0:T(8,128)S(1)}, f32[12,24,24]{2,1,0:T(8,128)}, u32[]{:S(2)}) copy-start(f32[12,24,24]{2,1,0:T(8,128)} %copy-done.1) | copy-start | bytes 82948
  70.7 1.8 %copy-start.4 = (f32[12,24,24]{2,1,0:T(8,128)S(1)}, f32[12,24,24]{2,1,0:T(8,128)}, u32[]{:S(2)}) copy-start(f32[12,24,24]{2,1,0:T(8,128)} %copy-done.3) | copy-start | bytes 82948
  71.8 0.8 copy-start.5
Sparse Core Ops, SparseCore 0:
  77.0 46.4 all-reduce.13
where the time goes:
time: 133 us; the launch traced here: 132 us
  waiting for transfers between devices  56.4 us (42%)
  between operations  20.5 us (15%)
  starting transfers between devices  17.2 us (13%)
  local copies, waits for them, and re-layouts  16.5 us (12%)
  matrix products  14.1 us (11%)
  other arithmetic  7.17 us (5%)
    psum x1, waiting for transfers between devices, shards(): return lax.psum(local_terms, 'cond')  46.6 us
    ppermute x2, starting transfers between devices, extended(): lax.ppermute(lax.slice_in_dim(block, block.shape[dim] - width, None, axis...  14.6 us
    dot_general x12, matrix products, highest(): jnp.dot(left_side, right_side, precision=lax.Precision.HIGHEST, preferred...  14.1 us
    ppermute x2, waiting for transfers between devices, extended(): lax.ppermute(lax.slice_in_dim(block, 0, width, axis=dim), axis, backward)  7.92 us
    reshape x2, local copies, waits for them, and re-layouts, tile_loss(): squared = (fields * fields).reshape(kernel_count, tile_size, 2, tile_size)  4.94 us
    reduce_sum x2, other arithmetic, tile_loss(): jnp.sum(squared, axis=(0, 2)) / (kernel_count * band_size * band_size)  3.94 us
  transfers between devices with their start and end apart: 5, of which 3 were waited for; matrix products, arithmetic and copies ran while one was open for 4% of the time, Pallas kernels for 0%

commit v1 on v0

--- a/solution.py
+++ b/solution.py
@@ -122,7 +122,7 @@
         dose_value = lax.dynamic_index_in_dim(dose, setting, 0, keepdims=False)
         summed = summed + jax.grad(tile_loss)(spectrum, kernel, dose_value, goal_map)
     local_terms = interior_adjoint(summed, tile_size, window_size)
-    return lax.psum(local_terms, "cond")
+    return jnp.sum(lax.all_gather(local_terms, "cond"), axis=0)
 
 
 def solution(mesh):

time: 133 us -> 82.5 us (0.62)
  the two profiles are of different devices: /device:TPU:1 before, /device:TPU:97 now
where the time goes in v1:
time: 82.5 us; the launch traced here: 81.9 us
  starting transfers between devices  19 us (23%)
  local copies, waits for them, and re-layouts  15 us (18%)
  matrix products  13.5 us (16%)
  waiting for transfers between devices  13 us (16%)
  other arithmetic  7.8 us (9%)
  between operations  7.16 us (9%)
  blocking collectives  6.35 us (8%)
    dot_general x12, matrix products, highest(): jnp.dot(left_side, right_side, precision=lax.Precision.HIGHEST, preferred...  13.5 us
    ppermute x2, starting transfers between devices, extended(): lax.ppermute(lax.slice_in_dim(block, block.shape[dim] - width, None, axis...  12.8 us
    ppermute x2, waiting for transfers between devices, extended(): lax.ppermute(lax.slice_in_dim(block, 0, width, axis=dim), axis, backward)  11.2 us
    all_gather x1, blocking collectives, shards(): return jnp.sum(lax.all_gather(local_terms, 'cond'), axis=0)  6.35 us
    ppermute x2, starting transfers between devices, extended(): lax.ppermute(lax.slice_in_dim(block, 0, width, axis=dim), axis, backward)  6.2 us
    reshape x2, local copies, waits for them, and re-layouts, tile_loss(): squared = (fields * fields).reshape(kernel_count, tile_size, 2, tile_size)  4.94 us
    reduce_sum x2, other arithmetic, tile_loss(): jnp.sum(squared, axis=(0, 2)) / (kernel_count * band_size * band_size)  3.94 us
    transpose x2, local copies, waits for them, and re-layouts, tile_loss(): jnp.transpose(stacked, (1, 0, 2))  1.86 us
  transfers between devices with their start and end apart: 4, of which 2 were waited for; matrix products, arithmetic and copies ran while one was open for 7% of the time, Pallas kernels for 0%

profile of v1, /device:TPU:97, one launch (start us, length us, event | category | flops | bytes accessed | tf_op | source)
XLA Modules:
  0.0 81.9 jit_solution(446252400515086727)
XLA Ops:
  0.0 3.1 %collective-permute-start = (f32[128,128]{1,0:T(8,128)}, f32[128,128]{1,0:T(8,128)S(1)}, u32[]{:S(2)}, u32[]{:S(2)}) collective-permute-start(f32[128,128]{1,0:T(8,128)} %param.5), channel_id=1, source_target_pairs={{0,32},{32,64},{64,96},{96,128},{128,160},{160,192},{192,224},{224... | collective-permute-start | bytes 196616 | tf_op jit(solution)/shard_map/ppermute | solution.py:18
  3.1 4.3 %collective-permute-start.1 = (f32[128,128]{1,0:T(8,128)}, f32[128,128]{1,0:T(8,128)S(1)}, u32[]{:S(2)}, u32[]{:S(2)}) collective-permute-start(f32[128,128]{1,0:T(8,128)} %param.5), channel_id=1, source_target_pairs={{32,0},{64,32},{96,64},{128,96},{160,128},{192,160},{224,192},{256... | collective-permute-start | bytes 196616 | tf_op jit(solution)/shard_map/ppermute | solution.py:21
  7.4 0.2 fusion.44
  7.7 0.1 fusion.77
  7.8 1.3 %fusion.100 = (s32[1]{0:T(128)}, s32[1]{0:T(128)}) fusion(s32[2]{0:T(128)} %param.7), kind=kLoop, calls=%fused_computation.146 | loop fusion | bytes 16 | tf_op jit(solution)/shard_map/slice | solution.py:120
  13.1 1.4 %fusion.99 = (f32[1]{0:T(128)}, f32[1]{0:T(128)}) fusion(f32[8]{0:T(128)} %param.9, s32[]{:T(128)S(6)} %select_n.60, s32[]{:T(128)S(6)} %select_n.63), kind=kLoop, calls=%fused_computation.145 | loop fusion | bytes 24 | tf_op jit(solution)/shard_map/jit(dynamic_index_in_dim)/dynamic_slice | solution.py:122
  17.2 1.3 %dynamic-slice_reduce_fusion.3 = (f32[12,576]{1,0:T(8,128)S(1)}, f32[12,576]{1,0:T(8,128)S(1)}, f32[12,576]{1,0:T(8,128)S(1)}, f32[12,576]{1,0:T(8,128)S(1)}) fusion(f32[8,2,12,576]{3,1,2,0:T(2,128)} %param.8, s32[]{:T(128)S(6)} %select_n.60, s32[]{:T(128)S(6)} %add.156, s32[]{:T(128)S(6)} %select_n.63), kind=kLoop, calls=%fused_computation.77 | loop fusion | bytes 221196 | tf_op jit(solution)/shard_map/jvp()/slice | solution.py:60
  18.5 0.1 squeeze.31
  18.6 0.1 squeeze.32
  18.7 0.1 squeeze.34
  18.8 0.1 squeeze.35
  19.0 0.8 %constant_dynamic-update-slice_fusion.1 = f32[384,128]{1,0:T(8,128)S(1)} fusion(f32[384,128]{1,0:T(8,128)S(1)} %constant_dynamic-update-slice_fusion.2, f32[128,128]{1,0:T(8,128)} %param.5), kind=kLoop, calls=%fused_computation.117 | loop fusion | bytes 131072
  19.8 9.7 %collective-permute-start.2 = (f32[384,128]{1,0:T(8,128)S(1)}, f32[384,128]{1,0:T(8,128)S(1)}, u32[]{:S(2)}, u32[]{:S(2)}) collective-permute-start(f32[384,128]{1,0:T(8,128)S(1)} %constant_dynamic-update-slice_fusion), channel_id=1, source_target_pairs={{0,2},{2,4},{4,6},{6,8},{8,10},{10,12},{12,14},{14,16},{16,18},{18... | collective-permute-start | bytes 589832 | tf_op jit(solution)/shard_map/ppermute | solution.py:18
  29.6 1.9 %collective-permute-start.3 = (f32[384,128]{1,0:T(8,128)S(1)}, f32[384,128]{1,0:T(8,128)S(1)}, u32[]{:S(2)}, u32[]{:S(2)}) collective-permute-start(f32[384,128]{1,0:T(8,128)S(1)} %constant_dynamic-update-slice_fusion), channel_id=1, source_target_pairs={{2,0},{4,2},{6,4},{8,6},{10,8},{12,10},{14,12},{16,14},{18,16},{20... | collective-permute-start | bytes 589832 | tf_op jit(solution)/shard_map/ppermute | solution.py:21
  31.5 0.1 fusion.79
  31.7 1.7 %collective-permute-done.2 = f32[384,128]{1,0:T(8,128)S(1)} collective-permute-done((f32[384,128]{1,0:T(8,128)S(1)}, f32[384,128]{1,0:T(8,128)S(1)}, u32[]{:S(2)}, u32[]{:S(2)}) %collective-permute-start.2) | collective-permute-done | bytes 196640 | tf_op jit(solution)/shard_map/ppermute | solution.py:18
  33.4 11.2 %collective-permute-done.3 = f32[384,128]{1,0:T(8,128)S(1)} collective-permute-done((f32[384,128]{1,0:T(8,128)S(1)}, f32[384,128]{1,0:T(8,128)S(1)}, u32[]{:S(2)}, u32[]{:S(2)}) %collective-permute-start.3) | collective-permute-done | bytes 196640 | tf_op jit(solution)/shard_map/ppermute | solution.py:21
  44.6 0.4 fusion.6
  45.1 0.2 fusion.32
  45.3 0.1 fusion.57
  45.4 0.1 multiply_subtract_fusion.1
  45.5 0.8 maximum_bitcast_fusion
  46.2 0.1 copy.35
  46.4 0.4 fusion.71
  46.9 2.6 %fusion.102 = (f32[1536,256]{1,0:T(8,128)}, f32[1536,256]{1,0:T(8,128)S(1)}) fusion(f32[24,128]{1,0:T(8,128)S(1)} %get-tuple-element.51, f32[24,128]{1,0:T(8,128)S(1)} %get-tuple-element.49, f32[24,128]{1,0:T(8,128)S(1)} %get-tuple-element.50, f32[6,8,12,128]{3,2,1,0:T(8,128)S(1)} %bitcast.86), kind=kOutput, calls=%fused_computation.148 | convolution fusion | flops 226922496 | bytes 3477504 | tf_op jit(solution)/shard_map/jvp()/dot_general | solution.py:27
  49.5 2.1 %reshape.142 = f32[12,128,2,128]{3,2,1,0:T(2,128)S(1)} reshape(f32[1536,256]{1,0:T(8,128)} %get-tuple-element.60) | data formatting | bytes 3145728 | tf_op jit(solution)/shard_map/jvp()/reshape | solution.py:89
  51.6 1.7 %copy.28 = f32[48,12,24]{0,2,1:T(8,128)} copy(f32[48,12,24]{2,0,1:T(8,128)} %get-tuple-element.62) | data formatting | bytes 110592 | tf_op jit(solution)/shard_map/jvp()/transpose | solution.py:65
  53.3 1.3 %fusion.72 = f32[256,288]{0,1:T(8,128)S(1)} fusion(f32[48,288]{0,1:T(8,128)} %bitcast.93, f32[128,24]{0,1:T(8,128)S(1)} %get-tuple-element.47, f32[128,24]{0,1:T(8,128)S(1)} %get-tuple-element.46, f32[128,24]{0,1:T(8,128)S(1)} %get-tuple-element.45), kind=kOutput, calls=%fused_computation.120 | convolution fusion | flops 42504192 | bytes 387072 | tf_op jit(solution)/shard_map/jvp()/dot_general | solution.py:27
  54.8 3.1 %fusion.101 = (f32[1536,256]{1,0:T(8,128)}, f32[1536,256]{1,0:T(8,128)}) fusion(f32[24,128]{1,0:T(8,128)S(1)} %get-tuple-element.51, f32[24,128]{1,0:T(8,128)S(1)} %get-tuple-element.49, f32[24,128]{1,0:T(8,128)S(1)} %get-tuple-element.50, f32[6,8,12,128]{3,2,1,0:T(8,128)S(1)} %bitcast.87), kind=kOutput, calls=%fused_computation.147 | convolution fusion | flops 226922496 | bytes 3477504 | tf_op jit(solution)/shard_map/jvp()/dot_general | solution.py:27
  57.9 2.9 %reshape.128 = f32[12,128,2,128]{3,2,1,0:T(2,128)} reshape(f32[1536,256]{1,0:T(8,128)} %get-tuple-element.58) | data formatting | bytes 3145728 | tf_op jit(solution)/shard_map/jvp()/reshape | solution.py:89
  60.8 1.3 %reduce_sum.105 = f32[128,128]{1,0:T(8,128)} reduce(f32[12,128,2,128]{3,2,1,0:T(2,128)S(1)} %reshape.142, f32[]{:T(128)} %constant.70.clone.1), dimensions={0,2}, to_apply=%region_5.6 | reduce | flops 376832 | bytes 1638404 | tf_op jit(solution)/shard_map/jvp()/reduce_sum | solution.py:90
  62.0 2.7 %reduce_sum.97 = f32[128,128]{1,0:T(8,128)} reduce(f32[12,128,2,128]{3,2,1,0:T(2,128)} %reshape.128, f32[]{:T(128)} %constant.70.clone.1), dimensions={0,2}, to_apply=%region_0.1 | reduce | flops 376832 | bytes 1638404 | tf_op jit(solution)/shard_map/jvp()/reduce_sum | solution.py:90
  64.7 1.6 %fusion.28 = (f32[128,128]{1,0:T(8,128)S(1)}, f32[128,128]{1,0:T(8,128)}) fusion(s32[128,128]{1,0:T(8,128)} %param.6, f32[128,128]{1,0:T(8,128)} %reduce_sum.97, f32[]{:T(128)} %bitcast.11, f32[]{:T(128)} %bitcast.10, f32[]{:T(128)} %bitcast.28, f32[128,128]{1,0:T(8,128)} %reduce_sum.105, f32[]{:T(128)} %bitcast.27), kind=kLoop, calls=%fused_computation.50 | loop fusion | flops 442368 | bytes 327696 | tf_op jit(solution)/shard_map/transpose(jvp())/div | solution.py:90
  66.3 0.5 broadcast_in_dim.4
  66.9 2.5 %fusion.2 = f32[1536,48]{0,1:T(8,128)} fusion(f32[192,8,2,128]{3,2,1,0:T(2,128)S(1)} %bitcast.82, f32[1536,256]{1,0:T(8,128)S(1)} %copy-done, f32[24,128]{1,0:T(8,128)S(1)} %get-tuple-element.51, f32[24,128]{1,0:T(8,128)S(1)} %get-tuple-element.49, f32[24,128]{1,0:T(8,128)S(1)} %get-tuple-element.50), kind=kOutput, calls=%fused_computation.4 | convolution fusion | flops 227315712 | bytes 3477504 | tf_op jit(solution)/shard_map/transpose(jvp())/dot_general | solution.py:27
  69.3 1.1 %reshape.130 = f32[12,128,48]{1,0,2:T(8,128)S(1)} reshape(f32[1536,48]{0,1:T(8,128)} %fusion.2) | data formatting | bytes 589824 | tf_op jit(solution)/shard_map/transpose(jvp())/reshape | solution.py:80
  70.5 0.4 fusion.22
  70.9 0.1 copy.34
  71.1 0.1 multiply_reduce_fusion.7
  71.2 0.5 broadcast_in_dim.5
  71.8 1.7 %fusion = f32[1536,48]{0,1:T(8,128)S(1)} fusion(f32[192,8,2,128]{3,2,1,0:T(2,128)S(1)} %bitcast.83, f32[1536,256]{1,0:T(8,128)S(1)} %get-tuple-element.61, f32[24,128]{1,0:T(8,128)S(1)} %get-tuple-element.51, f32[24,128]{1,0:T(8,128)S(1)} %get-tuple-element.49, f32[24,128]{1,0:T(8,128)S(1)} %get-tuple-element.50), kind=kOutput, calls=%fused_computation.1 | convolution fusion | flops 227315712 | bytes 3477504 | tf_op jit(solution)/shard_map/transpose(jvp())/dot_general | solution.py:27
  73.7 0.4 fusion.18
  74.1 0.1 copy.41
  74.3 0.1 multiply_reduce_fusion.3
  74.4 0.2 fusion.35
  74.6 0.3 convolution_multiply_fusion
  74.9 6.3 %all-gather = f32[256,128]{1,0:T(8,128)S(1)} all-gather(f32[128,128]{1,0:T(8,128)S(1)} %convolution_multiply_fusion), channel_id=2, replica_groups=mesh['row'=16,'col'=16,'cond'=2] {'cond'}, dimensions={0}, use_global_device_ids=true | all-gather | bytes 196608 | tf_op jit(solution)/shard_map/all_gather | solution.py:125
  81.2 0.6 reduce_sum.113
  (38 shorter events, 0.7 us)
Async XLA Ops:
  0.0 19.0 %collective-permute-start = (f32[128,128]{1,0:T(8,128)}, f32[128,128]{1,0:T(8,128)S(1)}, u32[]{:S(2)}, u32[]{:S(2)}) collective-permute-start(f32[128,128]{1,0:T(8,128)} %param.5), channel_id=1, source_target_pairs={{0,32},{32,64},{64,96},{96,128},{128,160},{160,192},{192,224},{224... | collective-permute-start | bytes 196616 | tf_op jit(solution)/shard_map/ppermute | solution.py:18
  3.1 16.7 %collective-permute-start.1 = (f32[128,128]{1,0:T(8,128)}, f32[128,128]{1,0:T(8,128)S(1)}, u32[]{:S(2)}, u32[]{:S(2)}) collective-permute-start(f32[128,128]{1,0:T(8,128)} %param.5), channel_id=1, source_target_pairs={{32,0},{64,32},{96,64},{128,96},{160,128},{192,160},{224,192},{256... | collective-permute-start | bytes 196616 | tf_op jit(solution)/shard_map/ppermute | solution.py:21
  18.6 26.9 %copy-start.1 = (f32[12,24,24]{2,1,0:T(8,128)}, f32[12,24,24]{2,1,0:T(8,128)S(1)}, u32[]{:S(2)}) copy-start(f32[12,24,24]{2,1,0:T(8,128)S(1)} %squeeze.31) | copy-start | bytes 82948
  18.7 26.8 %copy-start.3 = (f32[12,24,24]{2,1,0:T(8,128)}, f32[12,24,24]{2,1,0:T(8,128)S(1)}, u32[]{:S(2)}) copy-start(f32[12,24,24]{2,1,0:T(8,128)S(1)} %squeeze.32) | copy-start | bytes 82948
  19.8 13.6 %collective-permute-start.2 = (f32[384,128]{1,0:T(8,128)S(1)}, f32[384,128]{1,0:T(8,128)S(1)}, u32[]{:S(2)}, u32[]{:S(2)}) collective-permute-start(f32[384,128]{1,0:T(8,128)S(1)} %constant_dynamic-update-slice_fusion), channel_id=1, source_target_pairs={{0,2},{2,4},{4,6},{6,8},{8,10},{10,12},{12,14},{14,16},{16,18},{18... | collective-permute-start | bytes 589832 | tf_op jit(solution)/shard_map/ppermute | solution.py:18
  29.6 15.0 %collective-permute-start.3 = (f32[384,128]{1,0:T(8,128)S(1)}, f32[384,128]{1,0:T(8,128)S(1)}, u32[]{:S(2)}, u32[]{:S(2)}) collective-permute-start(f32[384,128]{1,0:T(8,128)S(1)} %constant_dynamic-update-slice_fusion), channel_id=1, source_target_pairs={{2,0},{4,2},{6,4},{8,6},{10,8},{12,10},{14,12},{16,14},{18,16},{20... | collective-permute-start | bytes 589832 | tf_op jit(solution)/shard_map/ppermute | solution.py:21
  62.0 4.8 %copy-start = (f32[1536,256]{1,0:T(8,128)S(1)}, f32[1536,256]{1,0:T(8,128)}, u32[]{:S(2)}) copy-start(f32[1536,256]{1,0:T(8,128)} %get-tuple-element.59) | copy-start | bytes 4718596
  69.3 1.8 %copy-start.2 = (f32[12,24,24]{2,1,0:T(8,128)S(1)}, f32[12,24,24]{2,1,0:T(8,128)}, u32[]{:S(2)}) copy-start(f32[12,24,24]{2,1,0:T(8,128)} %copy-done.1) | copy-start | bytes 82948
  69.3 1.8 %copy-start.4 = (f32[12,24,24]{2,1,0:T(8,128)S(1)}, f32[12,24,24]{2,1,0:T(8,128)}, u32[]{:S(2)}) copy-start(f32[12,24,24]{2,1,0:T(8,128)} %copy-done.3) | copy-start | bytes 82948
  70.4 0.8 %copy-start.5 = (f32[128,128]{1,0:T(8,128)S(1)}, f32[128,128]{1,0:T(8,128)}, u32[]{:S(2)}) copy-start(f32[128,128]{1,0:T(8,128)} %get-tuple-element.34) | copy-start | bytes 196612
